TPU v7x, 32 devices: a whole 2x2x4 slice. The times are simulated.
32 devices in a mesh: replica: 8 (over y, x, core), shard: 4 (over z).
Axes of the slice: x: 2, y: 2, z: 4, core: 2. Of those that a mesh axis runs over, the one named last changes fastest.
Arguments:
- inputs: bfloat16 [8, 1024, 1024], P('replica', 'shard'), may hold values from -6 to 6
- out_grad: bfloat16 [8, 1024, 1024], P('replica', 'shard'), may hold values from -6 to 6
- segment_ids: int32 [8, 1024], P('replica'), may hold values from 0 to 2, never falling along the last dimension, each value on 1 to 512 neighbouring positions
- ln_gain_attn: bfloat16 [1024], P('shard'), may hold values from 0.5 to 1.5
- ln_bias_attn: bfloat16 [1024], P('shard'), may hold values from -3 to 3
- ln_gain_mlp: bfloat16 [1024], P('shard'), may hold values from 0.5 to 1.5
- ln_bias_mlp: bfloat16 [1024], P('shard'), may hold values from -3 to 3
- qkv_weight: bfloat16 [1024, 3072], P('shard'), may hold values from -0.1875 to 0.1875
- qkv_bias: bfloat16 [3072], P('shard'), may hold values from -3 to 3
- out_weight: bfloat16 [1024, 1024], P('shard'), may hold values from -0.75 to 0.75
- up_weight: bfloat16 [1024, 4096], P('shard'), may hold values from -0.1875 to 0.1875
- up_bias: bfloat16 [4096], P('shard'), may hold values from -3 to 3
- down_weight: bfloat16 [4096, 1024], P('shard'), may hold values from -0.09375 to 0.09375
- output_bias: bfloat16 [1024], P('shard'), may hold values from -3 to 3
Outputs:
- outputs: bfloat16 [8, 1024, 1024], P('replica', 'shard')
- in_grad: bfloat16 [8, 1024, 1024], P('replica', 'shard')
- grad_ln_gain_attn: float32 [1024], P('shard')
- grad_ln_bias_attn: float32 [1024], P('shard')
- grad_ln_gain_mlp: float32 [1024], P('shard')
- grad_ln_bias_mlp: float32 [1024], P('shard')
- grad_qkv_weight: float32 [1024, 3072], P('shard')
- grad_qkv_bias: float32 [3072], P('shard')
- grad_out_weight: float32 [1024, 1024], P('shard')
- grad_up_weight: float32 [1024, 4096], P('shard')
- grad_up_bias: float32 [4096], P('shard')
- grad_down_weight: float32 [4096, 1024], P('shard')
- grad_output_bias: float32 [1024], P('shard')
Inputs may be any that keep to these rules, and one draw needn't show every extreme that they name: `segment_ids`: in every sequence the document numbers never fall and run through 0 to 2; every document has 1 to 512 tokens, one exactly 512.
All inputs are finite; a program needn't handle non-finite values.
Results may differ from a plain program's by a relative error of at most 0.012.
Values may be sent and summed in bfloat16 or wider, within the bound.
A program may use at most 256 MiB of HBM per device.

v0:
```python
from functools import partial
import jax
import jax.numpy as jnp
from jax import lax
from jax.sharding import PartitionSpec as P

D = 1024
FF = 4096
HEADS = 16
HEAD = 64
ROT = 16
DOCS = 3


def layer_norm(values, gain, shift):
    centered = values - jnp.mean(values, axis=-1, keepdims=True)
    variance = jnp.mean(centered * centered, axis=-1, keepdims=True)
    return centered * lax.rsqrt(variance + 1e-05) * gain + shift


def exact_gelu(values):
    return jax.nn.gelu(values, approximate=False)


def doc_positions(segment_row):
    documents = jnp.arange(DOCS, dtype=jnp.int32)
    member = (segment_row[:, None] == documents[None, :]).astype(jnp.int32)
    counts = jnp.sum(member, axis=0)
    starts = jnp.cumsum(counts) - counts
    doc_start = jnp.sum(member * starts[None, :], axis=1)
    return jnp.arange(segment_row.shape[0], dtype=jnp.int32) - doc_start


def rotate(features, positions):
    half_rot = ROT // 2
    inv_freq = 1.0 / 10000.0 ** (jnp.arange(half_rot, dtype=jnp.float32) * 2.0 / ROT)
    angles = positions.astype(jnp.float32)[..., None] * inv_freq
    cosine = jnp.cos(angles)[..., None, :]
    sine_part = jnp.sin(angles)[..., None, :]
    front_half = features[..., :half_rot]
    back_half = features[..., half_rot:ROT]
    return jnp.concatenate(
        [
            front_half * cosine - back_half * sine_part,
            back_half * cosine + front_half * sine_part,
            features[..., ROT:],
        ],
        axis=-1,
    )


def masked_scores(queries, key_rows, segment_row, first_row):
    local_len = queries.shape[0]
    query_at = first_row + jnp.arange(local_len, dtype=jnp.int32)
    key_at = jnp.arange(key_rows.shape[0], dtype=jnp.int32)
    query_doc = lax.dynamic_slice_in_dim(segment_row, first_row, local_len, 0)
    allowed = (key_at[None, :] <= query_at[:, None]) & (segment_row[None, :] == query_doc[:, None])
    score_scale = queries.shape[-1] ** (-0.5)
    scores = (
        jnp.einsum("qhd,khd->hqk", queries, key_rows, preferred_element_type=jnp.float32)
        * score_scale
    )
    return jnp.where(allowed[None], scores, -1e30)


def attend_forward(first_row, element):
    queries, key_rows, value_rows, segment_row = element
    scores = masked_scores(queries, key_rows, segment_row, first_row)
    row_max = jnp.max(scores, axis=-1, keepdims=True)
    shifted_exp = jnp.exp(scores - row_max)
    row_sum = jnp.sum(shifted_exp, axis=-1, keepdims=True)
    probs = (shifted_exp / row_sum).astype(jnp.bfloat16)
    context = jnp.einsum("hqk,khd->qhd", probs, value_rows, preferred_element_type=jnp.float32)
    return (context.astype(jnp.bfloat16), row_max + jnp.log(row_sum))


def attend_backward(first_row, element):
    queries, key_rows, value_rows, segment_row, log_norm, grad_context = element
    scores = masked_scores(queries, key_rows, segment_row, first_row)
    weights = jnp.exp(scores - log_norm)
    grad_probs = jnp.einsum(
        "qhd,khd->hqk", grad_context, value_rows, preferred_element_type=jnp.float32
    )
    row_inner = jnp.sum(weights * grad_probs, axis=-1, keepdims=True)
    grad_scores = (weights * (grad_probs - row_inner)).astype(jnp.bfloat16)
    score_scale = queries.shape[-1] ** (-0.5)
    grad_query = (
        jnp.einsum("hqk,khd->qhd", grad_scores, key_rows, preferred_element_type=jnp.float32)
        * score_scale
    )
    grad_key = (
        jnp.einsum("hqk,qhd->khd", grad_scores, queries, preferred_element_type=jnp.float32)
        * score_scale
    )
    grad_value = jnp.einsum(
        "hqk,qhd->khd",
        weights.astype(jnp.bfloat16),
        grad_context,
        preferred_element_type=jnp.float32,
    )
    return (grad_query, grad_key, grad_value)


def shards(
    inputs,
    out_grad,
    segment_ids,
    ln_gain_attn,
    ln_bias_attn,
    ln_gain_mlp,
    ln_bias_mlp,
    qkv_weight,
    qkv_bias,
    out_weight,
    up_weight,
    up_bias,
    down_weight,
    output_bias,
):
    seq_count, local_len, model_width = inputs.shape
    token_count = seq_count * local_len
    first_row = lax.axis_index("shard") * local_len
    group_ratio = FF // D
    flat_in = inputs.reshape(token_count, model_width).astype(jnp.float32)
    gain_attn, shift_attn, gain_mlp, shift_mlp, qkv_shift, up_shift, out_shift = (
        lax.all_gather(ln_gain_attn, "shard", axis=0, tiled=True),
        lax.all_gather(ln_bias_attn, "shard", axis=0, tiled=True),
        lax.all_gather(ln_gain_mlp, "shard", axis=0, tiled=True),
        lax.all_gather(ln_bias_mlp, "shard", axis=0, tiled=True),
        lax.all_gather(qkv_bias, "shard", axis=0, tiled=True),
        lax.all_gather(up_bias, "shard", axis=0, tiled=True),
        lax.all_gather(output_bias, "shard", axis=0, tiled=True),
    )
    attn_float, attn_pullback = jax.vjp(
        layer_norm, flat_in, gain_attn.astype(jnp.float32), shift_attn.astype(jnp.float32)
    )
    mlp_float, mlp_pullback = jax.vjp(
        layer_norm, flat_in, gain_mlp.astype(jnp.float32), shift_mlp.astype(jnp.float32)
    )
    attn_normed = attn_float.astype(jnp.bfloat16)
    mlp_normed = mlp_float.astype(jnp.bfloat16)
    pieces = (
        lax.all_gather(qkv_weight, "shard", axis=0, tiled=True),
        lax.all_gather(up_weight, "shard", axis=0, tiled=True),
    )
    qkv_sum = jnp.dot(attn_normed, pieces[0], preferred_element_type=jnp.float32)
    up_sum = jnp.dot(mlp_normed, pieces[1], preferred_element_type=jnp.float32)
    qkv_parts = (qkv_sum + qkv_shift.astype(jnp.float32)).reshape(
        seq_count, local_len, 3, HEADS, HEAD
    )
    all_positions = jax.vmap(doc_positions)(segment_ids)
    own_positions = lax.dynamic_slice_in_dim(all_positions, first_row, local_len, 1)

    def rotate_pair(query_part, key_part):
        return (rotate(query_part, own_positions), rotate(key_part, own_positions))

    (query_rot, key_rot), rotate_pullback = jax.vjp(
        rotate_pair, qkv_parts[:, :, 0], qkv_parts[:, :, 1]
    )
    query_low = query_rot.astype(jnp.bfloat16)
    key_low = key_rot.astype(jnp.bfloat16)
    value_low = qkv_parts[:, :, 2].astype(jnp.bfloat16)
    key_all, value_all = (
        lax.all_gather(key_low, "shard", axis=1, tiled=True),
        lax.all_gather(value_low, "shard", axis=1, tiled=True),
    )
    context_seq, log_norms = lax.map(
        partial(attend_forward, first_row), (query_low, key_all, value_all, segment_ids)
    )
    context_low = context_seq.reshape(token_count, model_width)
    hidden_act, gelu_pullback = jax.vjp(exact_gelu, up_sum + up_shift.astype(jnp.float32))
    hidden_low = hidden_act.astype(jnp.bfloat16)
    down_grouped = down_weight.reshape(-1, group_ratio * model_width)
    pieces = (
        lax.all_gather(out_weight, "shard", axis=0, tiled=True),
        lax.all_gather(down_grouped, "shard", axis=0, tiled=True),
    )
    piece_rows = pieces[0].shape[0]
    down_rows = pieces[1].reshape(piece_rows * group_ratio, model_width)
    mixed = jnp.dot(context_low, pieces[0], preferred_element_type=jnp.float32) + jnp.dot(
        hidden_low, down_rows, preferred_element_type=jnp.float32
    )
    result = flat_in + mixed + out_shift.astype(jnp.float32)
    outputs = result.astype(jnp.bfloat16).reshape(seq_count, local_len, model_width)
    grad_low = out_grad.reshape(token_count, model_width)
    grad_float = grad_low.astype(jnp.float32)
    grad_out_shift = jnp.sum(grad_float, axis=0)
    grad_out_weight = jnp.einsum(
        "tk,tn->kn", context_low, grad_low, preferred_element_type=jnp.float32
    )
    grad_down_weight = jnp.einsum(
        "tk,tn->kn", hidden_low, grad_low, preferred_element_type=jnp.float32
    )
    out_shares = (
        lax.psum_scatter(grad_out_weight, "shard", scatter_dimension=0, tiled=True),
        lax.psum_scatter(grad_down_weight, "shard", scatter_dimension=0, tiled=True),
        lax.psum_scatter(grad_out_shift, "shard", scatter_dimension=0, tiled=True),
    )
    out_totals = lax.psum((out_shares[0], out_shares[1], out_shares[2]), "replica")
    pieces = (
        lax.all_gather(out_weight, "shard", axis=0, tiled=True),
        lax.all_gather(down_grouped, "shard", axis=0, tiled=True),
    )
    piece_rows = pieces[0].shape[0]
    down_rows = pieces[1].reshape(piece_rows * group_ratio, model_width)
    context_part = jnp.einsum("tn,kn->tk", grad_low, pieces[0], preferred_element_type=jnp.float32)
    hidden_part = jnp.einsum("tn,kn->tk", grad_low, down_rows, preferred_element_type=jnp.float32)
    context_grad_low = context_part.astype(jnp.bfloat16).reshape(seq_count, local_len, HEADS, HEAD)
    hidden_grad_low = gelu_pullback(hidden_part)[0].astype(jnp.bfloat16)
    key_back, value_back = (key_all, value_all)
    grad_query, key_part, value_part = lax.map(
        partial(attend_backward, first_row),
        (query_low, key_back, value_back, segment_ids, log_norms, context_grad_low),
    )
    grad_key, grad_value = (
        lax.psum_scatter(key_part, "shard", scatter_dimension=1, tiled=True),
        lax.psum_scatter(value_part, "shard", scatter_dimension=1, tiled=True),
    )
    query_pre, key_pre = rotate_pullback((grad_query, grad_key))
    grad_qkv = (
        jnp.stack([query_pre, key_pre, grad_value], axis=2)
        .reshape(token_count, 3 * model_width)
        .astype(jnp.bfloat16)
    )
    grad_qkv_shift = jnp.sum(grad_qkv.astype(jnp.float32), axis=0)
    grad_up_shift = jnp.sum(hidden_grad_low.astype(jnp.float32), axis=0)
    grad_qkv_weight = jnp.einsum(
        "tk,tn->kn", attn_normed, grad_qkv, preferred_element_type=jnp.float32
    )
    grad_up_weight = jnp.einsum(
        "tk,tn->kn", mlp_normed, hidden_grad_low, preferred_element_type=jnp.float32
    )
    pieces = (
        lax.all_gather(qkv_weight, "shard", axis=0, tiled=True),
        lax.all_gather(up_weight, "shard", axis=0, tiled=True),
    )
    attn_part = jnp.einsum("tn,kn->tk", grad_qkv, pieces[0], preferred_element_type=jnp.float32)
    mlp_part = jnp.einsum(
        "tn,kn->tk", hidden_grad_low, pieces[1], preferred_element_type=jnp.float32
    )
    attn_input, grad_gain_attn, grad_shift_attn = attn_pullback(attn_part)
    mlp_input, grad_gain_mlp, grad_shift_mlp = mlp_pullback(mlp_part)
    in_grad = (
        (grad_float + attn_input + mlp_input)
        .astype(jnp.bfloat16)
        .reshape(seq_count, local_len, model_width)
    )
    in_shares = (
        lax.psum_scatter(grad_gain_attn, "shard", scatter_dimension=0, tiled=True),
        lax.psum_scatter(grad_shift_attn, "shard", scatter_dimension=0, tiled=True),
        lax.psum_scatter(grad_gain_mlp, "shard", scatter_dimension=0, tiled=True),
        lax.psum_scatter(grad_shift_mlp, "shard", scatter_dimension=0, tiled=True),
        lax.psum_scatter(grad_qkv_weight, "shard", scatter_dimension=0, tiled=True),
        lax.psum_scatter(grad_qkv_shift, "shard", scatter_dimension=0, tiled=True),
        lax.psum_scatter(grad_up_weight, "shard", scatter_dimension=0, tiled=True),
        lax.psum_scatter(grad_up_shift, "shard", scatter_dimension=0, tiled=True),
    )
    in_totals = lax.psum(
        (
            in_shares[0],
            in_shares[1],
            in_shares[2],
            in_shares[3],
            in_shares[4],
            in_shares[5],
            in_shares[6],
            in_shares[7],
        ),
        "replica",
    )
    return (
        outputs,
        in_grad,
        in_totals[0],
        in_totals[1],
        in_totals[2],
        in_totals[3],
        in_totals[4],
        in_totals[5],
        out_totals[0],
        in_totals[6],
        in_totals[7],
        out_totals[1],
        out_totals[2],
    )


def solution(mesh):
    placed = (
        P("replica", "shard", None),
        P("replica", "shard", None),
        P("replica", None),
        P("shard"),
        P("shard"),
        P("shard"),
        P("shard"),
        P("shard", None),
        P("shard"),
        P("shard", None),
        P("shard", None),
        P("shard"),
        P("shard", None),
        P("shard"),
    )
    return jax.shard_map(
        shards,
        mesh=mesh,
        in_specs=placed,
        out_specs=(
            P("replica", "shard", None),
            P("replica", "shard", None),
            P("shard"),
            P("shard"),
            P("shard"),
            P("shard"),
            P("shard", None),
            P("shard"),
            P("shard", None),
            P("shard", None),
            P("shard"),
            P("shard", None),
            P("shard"),
        ),
        check_vma=False,
    )
```

profile of v0, /device:TPU:0, one launch (start us, length us, event | category | flops | bytes accessed | tf_op | source)
XLA Modules:
  0.0 1781.5 jit_solution(8662586912904173164)
XLA Ops:
  9.4 14.7 all-gather.3
  24.8 11.0 all-gather.2
  50.4 77.4 %all-gather.14.cloned.1.call-done = bf16[1024,3072]{1,0:T(8,128)(2,1)} async-done(((bf16[256,3072]{1,0:T(8,128)(2,1)}), bf16[1024,3072]{1,0:T(8,128)(2,1)}) %all-gather.14.cloned.1.call-update) | async-done | bytes 6291472 | tf_op jit(solution)/shard_map/all_gather | solution.py:143
  146.5 27.0 %all-gather.18.cloned.1.call-done = bf16[1024,1024]{1,0:T(8,128)(2,1)} async-done(((bf16[256,1024]{1,0:T(8,128)(2,1)}), bf16[1024,1024]{1,0:T(8,128)(2,1)}) %all-gather.18.cloned.1.call-update) | async-done | bytes 2097168 | tf_op jit(solution)/shard_map/all_gather | solution.py:175
  177.3 43.3 %all-gather.16.cloned.1.call-done = bf16[1,1024,16,64]{1,3,2,0:T(8,128)(2,1)} async-done(((bf16[1,256,16,64]{1,3,2,0:T(8,128)(2,1)}), bf16[1,1024,16,64]{1,3,2,0:T(8,128)(2,1)}) %all-gather.16.cloned.1.call-update) | async-done | bytes 2097168 | tf_op jit(solution)/shard_map/all_gather | solution.py:164
  231.9 35.2 %all-gather.24.cloned.1.call-done = bf16[1,1024,1,16,64]{1,4,3,2,0:T(8,128)(2,1)} async-done(((bf16[1,256,1,16,64]{1,4,3,2,0:T(8,128)(2,1)}), bf16[1,1024,1,16,64]{1,4,3,2,0:T(8,128)(2,1)}) %all-gather.24.cloned.1.call-update) | async-done | bytes 2097168 | tf_op jit(solution)/shard_map/all_gather | solution.py:165
  267.2 15.4 multiply_reduce_fusion
  300.1 9.4 fusion.12
  322.9 14.4 all_gather.53
  346.1 11.3 all-gather.4
  357.5 59.8 %all-gather.22.cloned.1.call-done = bf16[1024,4096]{1,0:T(8,128)(2,1)} async-done(((bf16[256,4096]{1,0:T(8,128)(2,1)}), bf16[1024,4096]{1,0:T(8,128)(2,1)}) %all-gather.22.cloned.1.call-update) | async-done | bytes 8388624 | tf_op jit(solution)/shard_map/all_gather | solution.py:176
  417.3 14.2 reshape.567
  431.5 135.1 %all-gather.20.cloned.1.call-done = bf16[1024,4096]{1,0:T(8,128)(2,1)} async-done(((bf16[256,4096]{1,0:T(8,128)(2,1)}), bf16[1024,4096]{1,0:T(8,128)(2,1)}) %all-gather.20.cloned.1.call-update) | async-done | bytes 8388624 | tf_op jit(solution)/shard_map/all_gather | solution.py:144
  566.6 15.8 multiply_convert_fusion.1
  616.7 27.2 %reduce-scatter.7.cloned.1.call-done = f32[1,256,16,64]{1,3,2,0:T(8,128)} async-done(((f32[1,1024,16,64]{1,3,2,0:T(8,128)}), f32[1,256,16,64]{1,3,2,0:T(8,128)}) %reduce-scatter.7.cloned.1.call-update) | async-done | bytes 1048592 | tf_op jit(solution)/shard_map/reduce_scatter | solution.py:216
  647.3 76.4 %reduce-scatter.9.cloned.1.call-done = f32[1,256,16,64]{1,3,2,0:T(8,128)} async-done(((f32[1,1024,16,64]{1,3,2,0:T(8,128)}), f32[1,256,16,64]{1,3,2,0:T(8,128)}) %reduce-scatter.9.cloned.1.call-update) | async-done | bytes 1048592 | tf_op jit(solution)/shard_map/reduce_scatter | solution.py:217
  733.2 70.0 %reduce-scatter.13.cloned.1.call-done = f32[256,1024]{1,0:T(8,128)} async-done(((f32[1024,1024]{1,0:T(8,128)}), f32[256,1024]{1,0:T(8,128)}) %reduce-scatter.13.cloned.1.call-update) | async-done | bytes 1048592 | tf_op jit(solution)/shard_map/reduce_scatter | solution.py:195
  803.2 283.2 %reduce-scatter.15.cloned.1.call-done = f32[256,4096]{1,0:T(8,128)} async-done(((f32[1024,4096]{1,0:T(8,128)}), f32[256,4096]{1,0:T(8,128)}) %reduce-scatter.15.cloned.1.call-update) | async-done | bytes 4194320 | tf_op jit(solution)/shard_map/reduce_scatter | solution.py:255
  1086.4 283.4 %reduce-scatter.17.cloned.1.call-done = f32[1024,1024]{1,0:T(8,128)} async-done(((f32[4096,1024]{1,0:T(8,128)}), f32[1024,1024]{1,0:T(8,128)}) %reduce-scatter.17.cloned.1.call-update) | async-done | bytes 4194320 | tf_op jit(solution)/shard_map/reduce_scatter | solution.py:196
  1369.8 214.9 %reduce-scatter.11.cloned.1.call-done = f32[256,3072]{1,0:T(8,128)} async-done(((f32[1024,3072]{1,0:T(8,128)}), f32[256,3072]{1,0:T(8,128)}) %reduce-scatter.11.cloned.1.call-update) | async-done | bytes 3145744 | tf_op jit(solution)/shard_map/reduce_scatter | solution.py:253
  1585.4 10.9 all-gather.6
  1622.1 16.8 all-reduce.15
  1639.3 23.6 %all-reduce.13 = (f32[256]{0:T(256)}, f32[256]{0:T(256)}, f32[256]{0:T(256)}, f32[256]{0:T(256)}, f32[768]{0:T(1024)}, /*index=5*/f32[1024]{0:T(1024)}, f32[256]{0:T(256)}) all-reduce(f32[256]{0:T(256)S(1)} %dynamic-slice.3, f32[256]{0:T(256)S(1)} %dynamic-slice.5, ...), channel_id=1, replica_groups=mesh['replica'=8,'shard'=4] {'replica'}, use_global_device_ids=true, to_apply=%region_16.17 | all-reduce | flops 3072 | bytes 24576 | tf_op jit(solution)/shard_map/psum | solution.py:258
  1662.9 101.0 %all-reduce.18.cloned.1.call-done = (f32[256,3072]{1,0:T(8,128)}, f32[256,1024]{1,0:T(8,128)}, f32[256,4096]{1,0:T(8,128)}, f32[1024,1024]{1,0:T(8,128)}) async-done(((f32[256,3072]{1,0:T(8,128)}, f32[256,1024]{1,0:T(8,128)}, f32[256,4096]{1,0:T(8,128)}, f32[1024,1024]{1,0:T(8,128)}), (f32[256,3072]{1,0:T(8,128)}, f32[256,1024]{1,0:T(8,128)}, f32[256,4096]{1,0:T(8,128)}, ...) | async-done | bytes 12582928 | tf_op jit(solution)/shard_map/psum | solution.py:258
  (206 shorter events, 173.2 us)
Async XLA Ops:
  7.2 120.6 %all-gather.14.cloned.1.call-start = ((), (), s32[]{:S(2)}) async-start(), calls=%async_computation.6 | async-start | bytes 7864320 | tf_op jit(solution)/shard_map/all_gather | solution.py:143
  7.9 165.6 %all-gather.18.cloned.1.call-start = ((), (), s32[]{:S(2)}) async-start(), calls=%async_computation.8 | async-start | bytes 2621440 | tf_op jit(solution)/shard_map/all_gather | solution.py:175
  8.7 212.0 %all-gather.16.cloned.1.call-start = ((), (), s32[]{:S(2)}) async-start(), calls=%async_computation.7 | async-start | bytes 2621440 | tf_op jit(solution)/shard_map/all_gather | solution.py:164
  50.3 84.1 %copy-start.37 = (f32[256]{0:T(256)}, f32[256]{0:T(256)S(1)}, u32[]{:S(2)}) copy-start(f32[256]{0:T(256)S(1)} %fusion.53) | copy-start | bytes 3076
  50.3 84.1 %copy-start.32 = (f32[256]{0:T(256)}, f32[256]{0:T(256)S(1)}, u32[]{:S(2)}) copy-start(f32[256]{0:T(256)S(1)} %fusion.89) | copy-start | bytes 3076
  50.4 86.7 %copy-start.28 = (f32[256,8]{0,1:T(8,128)}, f32[256,8]{0,1:T(8,128)S(1)}, u32[]{:S(2)}) copy-start(f32[256,8]{0,1:T(8,128)S(1)} %get-tuple-element.122) | copy-start | bytes 24580
  50.4 86.7 %copy-start.29 = (f32[256,8]{0,1:T(8,128)}, f32[256,8]{0,1:T(8,128)S(1)}, u32[]{:S(2)}) copy-start(f32[256,8]{0,1:T(8,128)S(1)} %get-tuple-element.123) | copy-start | bytes 24580
  139.6 127.6 %all-gather.24.cloned.1.call-start = ((), (), s32[]{:S(2)}) async-start(), calls=%async_computation.17 | async-start | bytes 2621440 | tf_op jit(solution)/shard_map/all_gather | solution.py:165
  140.5 33.0 %copy-start.5 = (bf16[1,256,1024]{2,1,0:T(8,128)(2,1)S(1)}, bf16[1,256,1024]{2,1,0:T(8,128)(2,1)}, u32[]{:S(2)}) copy-start(bf16[1,256,1024]{2,1,0:T(8,128)(2,1)} %param.15) | copy-start | bytes 1572868
  140.5 276.7 %all-gather.22.cloned.1.call-start = ((), (), s32[]{:S(2)}) async-start(), calls=%async_computation.10 | async-start | bytes 10485760 | tf_op jit(solution)/shard_map/all_gather | solution.py:176
  145.0 75.6 %copy-start.21 = (bf16[256,16,8]{0,2,1:T(8,128)(2,1)S(1)}, bf16[256,16,8]{0,2,1:T(8,128)(2,1)}, u32[]{:S(2)}) copy-start(bf16[256,16,8]{0,2,1:T(8,128)(2,1)} %get-tuple-element.110) | copy-start | bytes 196612
  145.0 75.6 %copy-start.23 = (bf16[256,16,8]{0,2,1:T(8,128)(2,1)S(1)}, bf16[256,16,8]{0,2,1:T(8,128)(2,1)}, u32[]{:S(2)}) copy-start(bf16[256,16,8]{0,2,1:T(8,128)(2,1)} %get-tuple-element.111) | copy-start | bytes 196612
  145.0 421.6 %all-gather.20.cloned.1.call-start = ((), (), s32[]{:S(2)}) async-start(), calls=%async_computation.9 | async-start | bytes 10485760 | tf_op jit(solution)/shard_map/all_gather | solution.py:144
  145.6 498.3 %reduce-scatter.7.cloned.1.call-start = ((), (), s32[]{:S(2)}) async-start(), calls=%async_computation.11 | async-start | bytes 5242880 | tf_op jit(solution)/shard_map/reduce_scatter | solution.py:216
  177.3 47.9 %copy-start.12 = (bf16[256,16,48]{0,2,1:T(8,128)(2,1)}, bf16[256,16,48]{0,2,1:T(8,128)(2,1)S(1)}, u32[]{:S(2)}) copy-start(bf16[256,16,48]{0,2,1:T(8,128)(2,1)S(1)} %fusion.83) | copy-start | bytes 1179652
  299.4 424.2 %reduce-scatter.9.cloned.1.call-start = ((), (), s32[]{:S(2)}) async-start(), calls=%async_computation.12 | async-start | bytes 5242880 | tf_op jit(solution)/shard_map/reduce_scatter | solution.py:217
  309.6 493.6 %reduce-scatter.13.cloned.1.call-start = ((), (), s32[]{:S(2)}) async-start(), calls=%async_computation.14 | async-start | bytes 5242880 | tf_op jit(solution)/shard_map/reduce_scatter | solution.py:195
  322.3 764.1 %reduce-scatter.15.cloned.1.call-start = ((), (), s32[]{:S(2)}) async-start(), calls=%async_computation.15 | async-start | bytes 20971520 | tf_op jit(solution)/shard_map/reduce_scatter | solution.py:255
  357.5 209.2 %copy-start.2 = (bf16[1,256,1024]{2,1,0:T(8,128)(2,1)S(1)}, bf16[1,256,1024]{2,1,0:T(8,128)(2,1)}, u32[]{:S(2)}) copy-start(bf16[1,256,1024]{2,1,0:T(8,128)(2,1)} %param.14) | copy-start | bytes 1572868
  357.5 209.2 %copy-start.33 = (f32[256]{0:T(256)S(1)}, f32[256]{0:T(256)}, u32[]{:S(2)}) copy-start(f32[256]{0:T(256)} %copy-done.32) | copy-start | bytes 3076
  599.7 770.1 %reduce-scatter.17.cloned.1.call-start = ((), (), s32[]{:S(2)}) async-start(), calls=%async_computation.16 | async-start | bytes 20971520 | tf_op jit(solution)/shard_map/reduce_scatter | solution.py:196
  608.2 976.6 %reduce-scatter.11.cloned.1.call-start = ((), (), s32[]{:S(2)}) async-start(), calls=%async_computation.13 | async-start | bytes 15728640 | tf_op jit(solution)/shard_map/reduce_scatter | solution.py:253
  616.7 29.7 %slice-start.4 = ((f32[1,256,16,64]{1,3,2,0:T(8,128)}), f32[1,256,16,48]{1,3,2,0:T(8,128)S(1)}, s32[]{:S(2)}) async-start(f32[1,256,16,64]{1,3,2,0:T(8,128)} %copy-done.9), calls=%async_computation.23 | async-start | bytes 1572864 | tf_op jit(solution)/shard_map/transpose(jvp())/split | solution.py:42
  733.2 1030.8 %all-reduce.18.cloned.1.call-start = ((), (), s32[]{:S(2)}) async-start(), calls=%async_computation.18 | async-start | bytes 25165824 | tf_op jit(solution)/shard_map/psum | solution.py:258
  (39 other events, 268.2 us)
Sparse Core Ops, SparseCore 0:
  9.6 118.1 all-gather.13
  129.4 44.1 all-gather.17
  175.7 44.9 all-gather.15
  222.6 44.4 all-gather.23
  269.1 148.0 all-gather.21
  418.7 147.8 all-gather.19
  568.9 74.9 reduce-scatter.6
  646.3 77.2 reduce-scatter.8
  725.9 77.2 reduce-scatter.12
  805.6 280.7 reduce-scatter.14
  1088.8 281.0 reduce-scatter.16
  1372.2 212.5 reduce-scatter.10
  1589.3 174.6 all-reduce.17
where the time goes:
time: 1790 us; the launch traced here: 1780 us
  waiting for transfers between devices  1440 us (80%)
  matrix products  126 us (7%)
  blocking collectives  120 us (7%)
  local copies, waits for them, and re-layouts  55.4 us (3%)
  other arithmetic  26.3 us (1%)
    reduce_scatter x1, waiting for transfers between devices, shards(): lax.psum_scatter(grad_down_weight, 'shard', scatter_dimension=0, tiled=True)  283 us
    reduce_scatter x1, waiting for transfers between devices, shards(): lax.psum_scatter(grad_up_weight, 'shard', scatter_dimension=0, tiled=True)  283 us
    reduce_scatter x1, waiting for transfers between devices, shards(): lax.psum_scatter(grad_qkv_weight, 'shard', scatter_dimension=0, tiled=True)  215 us
    all_gather x1, waiting for transfers between devices, shards(): lax.all_gather(up_weight, 'shard', axis=0, tiled=True)  135 us
    psum x1, waiting for transfers between devices, shards(): lax.psum((in_shares[0], in_shares[1], in_shares[2], in_shares[3], in_shar...  101 us
    all_gather x1, waiting for transfers between devices, shards(): lax.all_gather(qkv_weight, 'shard', axis=0, tiled=True)  77.4 us
    reduce_scatter x1, waiting for transfers between devices, shards(): lax.psum_scatter(value_part, 'shard', scatter_dimension=1, tiled=True)  76.4 us
    reduce_scatter x1, waiting for transfers between devices, shards(): lax.psum_scatter(grad_out_weight, 'shard', scatter_dimension=0, tiled=True)  70 us
  transfers between devices with their start and end apart: 13, of which 13 were waited for; matrix products, arithmetic and copies ran while one was open for 10% of the time, Pallas kernels for 0%

commit v1 on v0

--- a/solution.py
+++ b/solution.py
@@ -10,6 +10,28 @@
 HEAD = 64
 ROT = 16
 DOCS = 3
+
+
+def in_order(blocks, dim):
+    blocks = jnp.moveaxis(blocks, 0, dim)
+    lengths = blocks.shape
+    return blocks.reshape(*lengths[:dim], lengths[dim] * lengths[dim + 1], *lengths[dim + 2 :])
+
+
+def ring_gather(x, axis, dim):
+    size = lax.axis_size(axis)
+    pairs = [(i, (i + 1) % size) for i in range(size)]
+    back = [(b, a) for a, b in pairs]
+    lower, upper = ([], [])
+    for step in range(size - 1):
+        if step % 2 == 0:
+            lower.append(lax.ppermute(lower[-1] if lower else x, axis, pairs))
+        else:
+            upper.append(lax.ppermute(upper[-1] if upper else x, axis, back))
+    pieces = jnp.stack([*lower[::-1], x, *upper])
+    shift = lax.axis_index(axis) - len(lower)
+    pieces = pieces[(jnp.arange(size) - shift) % size]
+    return in_order(pieces, dim)
 
 
 def layer_norm(values, gain, shift):
@@ -173,7 +195,7 @@
     down_grouped = down_weight.reshape(-1, group_ratio * model_width)
     pieces = (
         lax.all_gather(out_weight, "shard", axis=0, tiled=True),
-        lax.all_gather(down_grouped, "shard", axis=0, tiled=True),
+        ring_gather(down_grouped, "shard", 0),
     )
     piece_rows = pieces[0].shape[0]
     down_rows = pieces[1].reshape(piece_rows * group_ratio, model_width)

time: 1790 us -> 1910 us (1.067)
  blocking collectives: 120 us -> 261 us
  waiting for transfers between devices: 1440 us -> 1370 us
  local copies, waits for them, and re-layouts: 55.4 us -> 88 us
    all_gather x1, blocking collectives: 10.9 us -> 148 us  [shards(): lax.all_gather(output_bias, 'shard', axis=0, tiled=True)]
    ppermute x0 -> x3, waiting for transfers between devices: none -> 91.7 us  [the longest x2 91.7 us: ring_gather(): lower.append(lax.ppermute(lower[-1] if lower else x, axis, pairs))]
    reduce_scatter x1, waiting for transfers between devices: 70 us -> 0.02 us  [shards(): lax.psum_scatter(grad_out_weight, 'shard', scatter_dimension=0, tiled=True)]
    reduce_scatter x1, waiting for transfers between devices: 283 us -> 227 us  [shards(): lax.psum_scatter(grad_up_weight, 'shard', scatter_dimension=0, tiled=True)]
    psum x1, waiting for transfers between devices: 101 us -> 70.9 us  [shards(): lax.psum((in_shares[0], in_shares[1], in_shares[2], in_shares[3], in_shar...]
  transfers between devices with their start and end apart: 13 -> 16, of which waited for: 13 -> 13; matrix products, arithmetic and copies ran while one was open for 10% -> 12% of each run, Pallas kernels for 0% -> 0%
where the time goes in v1:
time: 1910 us; the launch traced here: 1900 us
  waiting for transfers between devices  1370 us (72%)
  blocking collectives  261 us (14%)
  matrix products  127 us (7%)
  local copies, waits for them, and re-layouts  88 us (5%)
  other arithmetic  37.3 us (2%)
    reduce_scatter x1, waiting for transfers between devices, shards(): lax.psum_scatter(grad_down_weight, 'shard', scatter_dimension=0, tiled=True)  283 us
    reduce_scatter x1, waiting for transfers between devices, shards(): lax.psum_scatter(grad_up_weight, 'shard', scatter_dimension=0, tiled=True)  227 us
    reduce_scatter x1, waiting for transfers between devices, shards(): lax.psum_scatter(grad_qkv_weight, 'shard', scatter_dimension=0, tiled=True)  215 us
    all_gather x1, blocking collectives, shards(): lax.all_gather(output_bias, 'shard', axis=0, tiled=True)  148 us
    all_gather x1, waiting for transfers between devices, shards(): lax.all_gather(up_weight, 'shard', axis=0, tiled=True)  135 us
    ppermute x2, waiting for transfers between devices, ring_gather(): lower.append(lax.ppermute(lower[-1] if lower else x, axis, pairs))  91.7 us
    reduce_scatter x1, waiting for transfers between devices, shards(): lax.psum_scatter(value_part, 'shard', scatter_dimension=1, tiled=True)  78.2 us
    all_gather x1, waiting for transfers between devices, shards(): lax.all_gather(qkv_weight, 'shard', axis=0, tiled=True)  77.3 us
  transfers between devices with their start and end apart: 16, of which 13 were waited for; matrix products, arithmetic and copies ran while one was open for 12% of the time, Pallas kernels for 0%

profile of v1, /device:TPU:0, one launch (start us, length us, event | category | flops | bytes accessed | tf_op | source)
XLA Modules:
  0.0 1903.6 jit_solution(11055341235827318222)
XLA Ops:
  9.4 12.6 all-gather.1
  31.1 13.7 all-gather.3
  50.6 77.3 %all-gather.14.cloned.1.call-done = bf16[1024,3072]{1,0:T(8,128)(2,1)} async-done(((bf16[256,3072]{1,0:T(8,128)(2,1)}), bf16[1024,3072]{1,0:T(8,128)(2,1)}) %all-gather.14.cloned.1.call-update) | async-done | bytes 6291472 | tf_op jit(solution)/shard_map/all_gather | solution.py:165
  146.6 27.1 %all-gather.18.cloned.1.call-done = bf16[1024,1024]{1,0:T(8,128)(2,1)} async-done(((bf16[256,1024]{1,0:T(8,128)(2,1)}), bf16[1024,1024]{1,0:T(8,128)(2,1)}) %all-gather.18.cloned.1.call-update) | async-done | bytes 2097168 | tf_op jit(solution)/shard_map/all_gather | solution.py:197
  177.5 43.3 %all-gather.16.cloned.1.call-done = bf16[1,1024,16,64]{1,3,2,0:T(8,128)(2,1)} async-done(((bf16[1,256,16,64]{1,3,2,0:T(8,128)(2,1)}), bf16[1,1024,16,64]{1,3,2,0:T(8,128)(2,1)}) %all-gather.16.cloned.1.call-update) | async-done | bytes 2097168 | tf_op jit(solution)/shard_map/all_gather | solution.py:186
  232.1 35.2 %all-gather.24.cloned.1.call-done = bf16[1,1024,1,16,64]{1,4,3,2,0:T(8,128)(2,1)} async-done(((bf16[1,256,1,16,64]{1,4,3,2,0:T(8,128)(2,1)}), bf16[1,1024,1,16,64]{1,4,3,2,0:T(8,128)(2,1)}) %all-gather.24.cloned.1.call-update) | async-done | bytes 2097168 | tf_op jit(solution)/shard_map/all_gather | solution.py:187
  267.3 15.4 multiply_reduce_fusion
  331.5 13.9 all-gather.5
  345.5 14.9 all_gather.52
  360.3 56.5 %all-gather.22.cloned.1.call-done = bf16[1024,4096]{1,0:T(8,128)(2,1)} async-done(((bf16[256,4096]{1,0:T(8,128)(2,1)}), bf16[1024,4096]{1,0:T(8,128)(2,1)}) %all-gather.22.cloned.1.call-update) | async-done | bytes 8388624 | tf_op jit(solution)/shard_map/all_gather | solution.py:224
  416.9 14.3 reshape.617
  431.2 135.1 %all-gather.20.cloned.1.call-done = bf16[1024,4096]{1,0:T(8,128)(2,1)} async-done(((bf16[256,4096]{1,0:T(8,128)(2,1)}), bf16[1024,4096]{1,0:T(8,128)(2,1)}) %all-gather.20.cloned.1.call-update) | async-done | bytes 8388624 | tf_op jit(solution)/shard_map/all_gather | solution.py:166
  566.2 15.8 multiply_convert_fusion.1
  616.4 27.1 %reduce-scatter.7.cloned.1.call-done = f32[1,256,16,64]{1,3,2,0:T(8,128)} async-done(((f32[1,1024,16,64]{1,3,2,0:T(8,128)}), f32[1,256,16,64]{1,3,2,0:T(8,128)}) %reduce-scatter.7.cloned.1.call-update) | async-done | bytes 1048592 | tf_op jit(solution)/shard_map/reduce_scatter | solution.py:238
  645.0 78.2 %reduce-scatter.9.cloned.1.call-done = f32[1,256,16,64]{1,3,2,0:T(8,128)} async-done(((f32[1,1024,16,64]{1,3,2,0:T(8,128)}), f32[1,256,16,64]{1,3,2,0:T(8,128)}) %reduce-scatter.9.cloned.1.call-update) | async-done | bytes 1048592 | tf_op jit(solution)/shard_map/reduce_scatter | solution.py:239
  737.8 91.7 %collective-permute-done = bf16[256,4096]{1,0:T(8,128)(2,1)} collective-permute-done((bf16[256,4096]{1,0:T(8,128)(2,1)}, bf16[256,4096]{1,0:T(8,128)(2,1)}, u32[]{:S(2)}, u32[]{:S(2)}) %collective-permute-start) | collective-permute-done | bytes 2097184 | tf_op jit(solution)/shard_map/ppermute | solution.py:28
  834.6 147.6 %all-gather.6 = bf16[4,1,256]{2,1,0:T(2,128)(2,1)S(1)} all-gather(bf16[1,1,256]{2,1,0:T(2,128)(2,1)S(1)} %reshape.647), channel_id=1, replica_groups=mesh['replica'=8,'shard'=4] {'shard'}, dimensions={0}, use_global_device_ids=true | all-gather | bytes 2560 | tf_op jit(solution)/shard_map/all_gather | solution.py:154
  982.2 227.0 %reduce-scatter.15.cloned.1.call-done = f32[256,4096]{1,0:T(8,128)} async-done(((f32[1024,4096]{1,0:T(8,128)}), f32[256,4096]{1,0:T(8,128)}) %reduce-scatter.15.cloned.1.call-update) | async-done | bytes 4194320 | tf_op jit(solution)/shard_map/reduce_scatter | solution.py:277
  1209.2 282.8 %reduce-scatter.17.cloned.1.call-done = f32[1024,1024]{1,0:T(8,128)} async-done(((f32[4096,1024]{1,0:T(8,128)}), f32[1024,1024]{1,0:T(8,128)}) %reduce-scatter.17.cloned.1.call-update) | async-done | bytes 4194320 | tf_op jit(solution)/shard_map/reduce_scatter | solution.py:218
  1492.0 214.9 %reduce-scatter.11.cloned.1.call-done = f32[256,3072]{1,0:T(8,128)} async-done(((f32[1024,3072]{1,0:T(8,128)}), f32[256,3072]{1,0:T(8,128)}) %reduce-scatter.11.cloned.1.call-update) | async-done | bytes 3145744 | tf_op jit(solution)/shard_map/reduce_scatter | solution.py:275
  1734.8 14.4 reshape_reshape.3
  1772.6 18.9 all-reduce.15
  1791.9 23.3 %all-reduce.13 = (f32[256]{0:T(256)}, f32[256]{0:T(256)}, f32[256]{0:T(256)}, f32[256]{0:T(256)}, f32[768]{0:T(1024)}, /*index=5*/f32[1024]{0:T(1024)}, f32[256]{0:T(256)}) all-reduce(f32[256]{0:T(256)S(1)} %dynamic-slice.3, f32[256]{0:T(256)S(1)} %dynamic-slice.5, ...), channel_id=1, replica_groups=mesh['replica'=8,'shard'=4] {'replica'}, use_global_device_ids=true, to_apply=%region_16.17 | all-reduce | flops 3072 | bytes 24576 | tf_op jit(solution)/shard_map/psum | solution.py:280
  1815.2 70.9 %all-reduce.18.cloned.1.call-done = (f32[256,3072]{1,0:T(8,128)}, f32[256,1024]{1,0:T(8,128)}, f32[256,4096]{1,0:T(8,128)}, f32[1024,1024]{1,0:T(8,128)}) async-done(((f32[256,3072]{1,0:T(8,128)}, f32[256,1024]{1,0:T(8,128)}, f32[256,4096]{1,0:T(8,128)}, f32[1024,1024]{1,0:T(8,128)}), (f32[256,3072]{1,0:T(8,128)}, f32[256,1024]{1,0:T(8,128)}, f32[256,4096]{1,0:T(8,128)}, ...) | async-done | bytes 12582928 | tf_op jit(solution)/shard_map/psum | solution.py:280
  (229 shorter events, 215.0 us)
Async XLA Ops:
  7.2 120.7 %all-gather.14.cloned.1.call-start = ((), (), s32[]{:S(2)}) async-start(), calls=%async_computation.6 | async-start | bytes 7864320 | tf_op jit(solution)/shard_map/all_gather | solution.py:165
  7.9 165.8 %all-gather.18.cloned.1.call-start = ((), (), s32[]{:S(2)}) async-start(), calls=%async_computation.8 | async-start | bytes 2621440 | tf_op jit(solution)/shard_map/all_gather | solution.py:197
  8.7 212.1 %all-gather.16.cloned.1.call-start = ((), (), s32[]{:S(2)}) async-start(), calls=%async_computation.7 | async-start | bytes 2621440 | tf_op jit(solution)/shard_map/all_gather | solution.py:186
  50.4 84.0 %copy-start.41 = (f32[256]{0:T(256)}, f32[256]{0:T(256)S(1)}, u32[]{:S(2)}) copy-start(f32[256]{0:T(256)S(1)} %fusion.53) | copy-start | bytes 3076
  50.6 86.6 %copy-start.32 = (f32[256,8]{0,1:T(8,128)}, f32[256,8]{0,1:T(8,128)S(1)}, u32[]{:S(2)}) copy-start(f32[256,8]{0,1:T(8,128)S(1)} %get-tuple-element.124) | copy-start | bytes 24580
  50.6 86.6 %copy-start.33 = (f32[256,8]{0,1:T(8,128)}, f32[256,8]{0,1:T(8,128)S(1)}, u32[]{:S(2)}) copy-start(f32[256,8]{0,1:T(8,128)S(1)} %get-tuple-element.125) | copy-start | bytes 24580
  139.7 127.6 %all-gather.24.cloned.1.call-start = ((), (), s32[]{:S(2)}) async-start(), calls=%async_computation.17 | async-start | bytes 2621440 | tf_op jit(solution)/shard_map/all_gather | solution.py:187
  140.6 276.2 %all-gather.22.cloned.1.call-start = ((), (), s32[]{:S(2)}) async-start(), calls=%async_computation.12 | async-start | bytes 10485760 | tf_op jit(solution)/shard_map/all_gather | solution.py:224
  145.2 421.0 %all-gather.20.cloned.1.call-start = ((), (), s32[]{:S(2)}) async-start(), calls=%async_computation.9 | async-start | bytes 10485760 | tf_op jit(solution)/shard_map/all_gather | solution.py:166
  145.8 497.8 %reduce-scatter.7.cloned.1.call-start = ((), (), s32[]{:S(2)}) async-start(), calls=%async_computation.10 | async-start | bytes 5242880 | tf_op jit(solution)/shard_map/reduce_scatter | solution.py:238
  299.8 423.4 %reduce-scatter.9.cloned.1.call-start = ((), (), s32[]{:S(2)}) async-start(), calls=%async_computation.11 | async-start | bytes 5242880 | tf_op jit(solution)/shard_map/reduce_scatter | solution.py:239
  310.0 672.2 %reduce-scatter.13.cloned.1.call-start = ((), (), s32[]{:S(2)}) async-start(), calls=%async_computation.14 | async-start | bytes 5242880 | tf_op jit(solution)/shard_map/reduce_scatter | solution.py:217
  322.7 886.5 %reduce-scatter.15.cloned.1.call-start = ((), (), s32[]{:S(2)}) async-start(), calls=%async_computation.15 | async-start | bytes 20971520 | tf_op jit(solution)/shard_map/reduce_scatter | solution.py:277
  360.3 205.9 %copy-start.2 = (bf16[1,256,1024]{2,1,0:T(8,128)(2,1)S(1)}, bf16[1,256,1024]{2,1,0:T(8,128)(2,1)}, u32[]{:S(2)}) copy-start(bf16[1,256,1024]{2,1,0:T(8,128)(2,1)} %param.14) | copy-start | bytes 1572868
  360.3 205.9 %copy-start.37 = (f32[256]{0:T(256)S(1)}, f32[256]{0:T(256)}, u32[]{:S(2)}) copy-start(f32[256]{0:T(256)} %copy-done.36) | copy-start | bytes 3076
  599.4 892.6 %reduce-scatter.17.cloned.1.call-start = ((), (), s32[]{:S(2)}) async-start(), calls=%async_computation.16 | async-start | bytes 20971520 | tf_op jit(solution)/shard_map/reduce_scatter | solution.py:218
  607.8 1099.1 %reduce-scatter.11.cloned.1.call-start = ((), (), s32[]{:S(2)}) async-start(), calls=%async_computation.13 | async-start | bytes 15728640 | tf_op jit(solution)/shard_map/reduce_scatter | solution.py:275
  733.8 95.7 %copy-start.4 = (bf16[1024,1024]{1,0:T(8,128)(2,1)S(1)}, bf16[1024,1024]{1,0:T(8,128)(2,1)}, u32[]{:S(2)}) copy-start(bf16[1024,1024]{1,0:T(8,128)(2,1)} %param.26) | copy-start | bytes 6291460
  733.8 98.2 %copy-start.48 = (u32[32]{0:T(128)S(1)}, u32[32]{0:T(128)}, u32[]{:S(2)}) copy-start(u32[32]{0:T(128)} %constant.193) | copy-start | bytes 388
  733.9 100.7 %copy-start.47 = (bf16[256]{0:T(256)(128)(2,1)S(1)}, bf16[256]{0:T(256)(128)(2,1)}, u32[]{:S(2)}) copy-start(bf16[256]{0:T(256)(128)(2,1)} %param.27) | copy-start | bytes 1540
  733.9 1152.2 %all-reduce.18.cloned.1.call-start = ((), (), s32[]{:S(2)}) async-start(), calls=%async_computation.18 | async-start | bytes 25165824 | tf_op jit(solution)/shard_map/psum | solution.py:280
  733.9 95.6 %collective-permute-start = (bf16[256,4096]{1,0:T(8,128)(2,1)}, bf16[256,4096]{1,0:T(8,128)(2,1)}, u32[]{:S(2)}, u32[]{:S(2)}) collective-permute-start(bf16[256,4096]{1,0:T(8,128)(2,1)} %reshape.614), channel_id=1, source_target_pairs={{0,1},{1,2},{2,3},{3,0},{4,5},{5,6},{6,7},{7,4},{8,9},{9,10},{10,1... | collective-permute-start | bytes 6291464 | tf_op jit(solution)/shard_map/ppermute | solution.py:28
  735.4 971.5 %collective-permute-start.2 = (bf16[256,4096]{1,0:T(8,128)(2,1)}, bf16[256,4096]{1,0:T(8,128)(2,1)}, u32[]{:S(2)}, u32[]{:S(2)}) collective-permute-start(bf16[256,4096]{1,0:T(8,128)(2,1)} %reshape.614), channel_id=1, source_target_pairs={{1,0},{2,1},{3,2},{0,3},{5,4},{6,5},{7,6},{4,7},{9,8},{10,9},{11,1... | collective-permute-start | bytes 6291464 | tf_op jit(solution)/shard_map/ppermute | solution.py:30
  829.5 877.5 %collective-permute-start.1 = (bf16[256,4096]{1,0:T(8,128)(2,1)}, bf16[256,4096]{1,0:T(8,128)(2,1)}, u32[]{:S(2)}, u32[]{:S(2)}) collective-permute-start(bf16[256,4096]{1,0:T(8,128)(2,1)} %collective-permute-done), channel_id=1, source_target_pairs={{0,1},{1,2},{2,3},{3,0},{4,5},{5,6},{6,7},{7,4},{8,9},{9,10},{10,1... | collective-permute-start | bytes 6291464 | tf_op jit(solution)/shard_map/ppermute | solution.py:28
  (46 other events, 577.0 us)
Sparse Core Ops, SparseCore 0:
  9.6 118.2 all-gather.13
  129.4 44.1 all-gather.17
  175.8 44.9 all-gather.15
  222.8 44.4 all-gather.23
  268.7 148.0 all-gather.21
  418.3 147.8 all-gather.19
  568.5 74.9 reduce-scatter.6
  645.9 77.2 reduce-scatter.8
  725.5 154.1 reduce-scatter.12
  882.0 327.1 reduce-scatter.14
  1211.6 280.3 reduce-scatter.16
  1494.3 212.5 reduce-scatter.10
  1711.4 174.6 all-reduce.17
